TPU v7x, 32 devices: a whole 2x2x4 slice. The times are simulated.
32 devices in a mesh: blk: 8 (over z, x), layer: 4 (over y, core).
Axes of the slice: x: 2, y: 2, z: 4, core: 2. Of those that a mesh axis runs over, the one named last changes fastest.
Arguments:
- tile_values: bfloat16 [16, 4, 1, 128, 128], P('blk', 'layer'), may hold values from 0 to 10, as said below
- band_rows: int32 [16, 4, 1], P('blk', 'layer'), may hold values from 0 to 3, as said below
- kept_rows: int32 [16, 4, 4], P('blk', 'layer'), may hold values from 0 to 3, as said below
- prune_mask: int32 [16, 4, 128], P('blk'), may hold values 0 or 1
Outputs:
- kept: bfloat16 [16, 4, 4, 128, 128], P('blk', None, 'layer')
Inputs may be any that keep to these rules, and one draw needn't show every extreme that they name: `tile_values`: positive tile entries. `band_rows`: within each column panel and band the 1 block rows are distinct. `kept_rows`: within each column panel and band the 4 kept block rows are distinct.
All inputs are finite; a program needn't handle non-finite values. No bound on the sum of `prune_mask` on one device may be relied on, other than what follows from the above.
Results may differ from a plain program's by a relative error of at most 0.001.
Values may be sent and summed in bfloat16 or wider, within the bound.
A program may use at most 192 MiB of HBM per device.

v0:
```python
import jax
import jax.numpy as jnp
from jax import lax
from jax.sharding import PartitionSpec as P


def densify(packed, positions, block_count):
    slot_ids = jnp.arange(block_count, dtype=jnp.int32)
    select = (positions[:, None, :] == slot_ids[None, :, None]).astype(jnp.bfloat16)
    dense = jnp.einsum("nrk,nkab->nrab", select, packed, preferred_element_type=jnp.float32)
    return dense.astype(jnp.bfloat16)


def per_device(tile_values, band_rows, kept_rows, prune_mask):
    panels = tile_values.shape[0]
    per_band = tile_values.shape[2]
    tile_size = tile_values.shape[3]
    band_count = lax.axis_size("layer")
    cycle_size = lax.axis_size("blk")
    panel_count = panels * cycle_size
    band_blocks = panel_count // band_count
    gathered, gathered_rows = (
        lax.all_gather(tile_values, "layer", axis=1, tiled=True),
        lax.all_gather(band_rows, "layer", axis=1, tiled=True),
    )
    right_dense = densify(
        gathered.reshape(panels * band_count, per_band, tile_size, tile_size),
        gathered_rows.reshape(panels * band_count, per_band),
        band_blocks,
    )
    right_side = (
        right_dense.reshape(panels, panel_count, tile_size, tile_size)
        .transpose(1, 2, 0, 3)
        .reshape(panel_count * tile_size, panels * tile_size)
    )
    own_tiles = tile_values[:, 0]
    own_rows = band_rows[:, 0]
    dense_own = densify(own_tiles, own_rows, band_blocks)
    dense_left = lax.all_gather(dense_own, "blk", axis=0, tiled=True)
    piece_count = dense_left.shape[0]
    operand = right_side
    operand = operand.reshape(piece_count, tile_size, panels * tile_size)
    left_blocks = dense_left.reshape(piece_count, band_blocks * tile_size, tile_size)
    expanded = lax.dot_general(
        left_blocks, operand, (((0, 2), (0, 1)), ((), ())), preferred_element_type=jnp.float32
    )
    squared = expanded * expanded
    partial_value = jnp.sum(squared, axis=0)
    totals = lax.psum(partial_value, "layer")
    row_count = panel_count * tile_size
    scaled = (squared * (row_count / totals)).astype(jnp.bfloat16)
    kept_count = kept_rows.shape[2]
    per_layer = kept_count // band_count
    gathered_rows_all, every_kept = (
        lax.all_gather(scaled, "layer", axis=0, tiled=True),
        lax.all_gather(kept_rows, "layer", axis=1, tiled=True),
    )
    blocked = gathered_rows_all.reshape(panel_count, tile_size, panels, tile_size)
    layer_index = lax.axis_index("layer")
    own_slots = lax.dynamic_slice_in_dim(every_kept, layer_index * per_layer, per_layer, 2)
    target = own_slots + (jnp.arange(band_count, dtype=jnp.int32) * band_blocks)[None, :, None]
    select = (
        target[..., None] == jnp.arange(panel_count, dtype=jnp.int32)[None, None, None, :]
    ).astype(jnp.bfloat16)
    picked = jnp.einsum(
        "jqmr,rajc->jqmac", select, blocked, preferred_element_type=jnp.float32
    ).astype(jnp.bfloat16)
    keep_mask = prune_mask[:, :, None, None, :].astype(jnp.bfloat16)
    return picked * keep_mask


def solution(mesh):
    return jax.shard_map(
        per_device,
        mesh=mesh,
        in_specs=(
            P("blk", "layer", None, None, None),
            P("blk", "layer", None),
            P("blk", "layer", None),
            P("blk", None, None),
        ),
        out_specs=P("blk", None, "layer", None, None),
        check_vma=False,
    )
```

profile of v0, /device:TPU:0, one launch (start us, length us, event | category | flops | bytes accessed | tf_op | source)
XLA Modules:
  0.0 96.1 jit_solution(15783242523122236507)
XLA Ops:
  6.5 0.0 all-gather.3.cloned.1.call-start
  6.5 0.8 bitcast_convert_fusion.1
  7.4 0.7 compare_convert_fusion
  8.1 0.8 multiply_convert_fusion.2
  8.9 0.0 all-gather.3.cloned.1.call-update
  9.0 0.0 all-gather.5.cloned.1.call-start
  9.0 6.2 %all_gather.17 = s32[2,4,1]{0,2,1:T(1,128)S(1)} all-gather(s32[2,1,1]{0,2,1:T(1,128)} %param.5), channel_id=1, replica_groups=mesh['blk'=8,'layer'=4] {'layer'}, dimensions={1}, use_global_device_ids=true | all-gather | bytes 40 | tf_op jit(solution)/shard_map/all_gather | solution.py:24
  15.2 0.1 copy.25
  15.3 0.1 eq.62
  15.4 6.4 %all_gather.18 = bf16[2,4,1,128,128]{4,3,2,1,0:T(8,128)(2,1)S(1)} all-gather(bf16[2,1,1,128,128]{4,3,2,1,0:T(8,128)(2,1)} %param.4), channel_id=1, replica_groups=mesh['blk'=8,'layer'=4] {'layer'}, dimensions={1}, use_global_device_ids=true | all-gather | bytes 327680 | tf_op jit(solution)/shard_map/all_gather | solution.py:23
  21.8 0.1 fusion.6
  21.9 0.1 bitcast_convert_fusion
  21.9 0.2 multiply_convert_fusion
  22.2 0.7 copy.26
  22.8 38.7 %all-gather.3.cloned.1.call-done = bf16[16,4,128,128]{3,2,1,0:T(8,128)(2,1)} async-done(((bf16[2,4,128,128]{3,2,1,0:T(8,128)(2,1)}), bf16[16,4,128,128]{3,2,1,0:T(8,128)(2,1)}) %all-gather.3.cloned.1.call-update) | async-done | bytes 2097168 | tf_op jit(solution)/shard_map/all_gather | solution.py:39
  61.5 0.0 copy-start.1
  61.5 0.0 copy-start
  61.5 2.4 %fusion.8 = (f32[256]{0:T(256)S(1)}, f32[512,256]{1,0:T(8,128)S(1)}) fusion(bf16[16,512,128]{2,1,0:T(8,128)(2,1)} %bitcast.34, bf16[16,128,256]{1,2,0:T(8,128)(2,1)S(1)} %bitcast.31), kind=kOutput, calls=%fused_computation.21 | convolution fusion | flops 537132800 | bytes 3671040 | tf_op jit(solution)/shard_map/dot_general | solution.py:44
  63.9 5.7 %psum.7 = f32[256]{0:T(256)S(1)} all-reduce(f32[256]{0:T(256)S(1)} %get-tuple-element.5), channel_id=1, replica_groups=mesh['blk'=8,'layer'=4] {'layer'}, use_global_device_ids=true, to_apply=%region_1.0 | all-reduce | flops 256 | bytes 2048 | tf_op jit(solution)/shard_map/psum | solution.py:49
  69.6 0.8 multiply_convert_fusion.1
  70.3 0.0 all-gather.5.cloned.1.call-update
  70.3 0.0 copy-done.1
  70.3 5.1 %all_gather.15 = s32[2,4,4]{2,0,1:T(2,128)S(1)} all-gather(s32[2,1,4]{2,0,1:T(2,128)S(1)} %bitcast.32), channel_id=1, replica_groups=mesh['blk'=8,'layer'=4] {'layer'}, dimensions={1}, use_global_device_ids=true | all-gather | bytes 160 | tf_op jit(solution)/shard_map/all_gather | solution.py:56
  75.4 0.1 constant_dynamic-slice_fusion
  75.5 0.1 copy.32
  75.6 0.0 copy-done
  75.6 10.3 %all-gather.5.cloned.1.call-done = bf16[2048,256]{1,0:T(8,128)(2,1)} async-done(((bf16[512,256]{1,0:T(8,128)(2,1)}), bf16[2048,256]{1,0:T(8,128)(2,1)}) %all-gather.5.cloned.1.call-update) | async-done | bytes 1048592 | tf_op jit(solution)/shard_map/all_gather | solution.py:55
  86.0 1.3 %reshape.87 = bf16[16,128,2,128]{3,2,1,0:T(2,128)(2,1)S(1)} reshape(bf16[2048,256]{1,0:T(8,128)(2,1)} %all-gather.5.cloned.1.call-done) | data formatting | bytes 2097152 | tf_op jit(solution)/shard_map/reshape | solution.py:58
  87.3 1.2 %fusion.2 = bf16[2,4,1,128,128]{4,1,3,0,2:T(4,128)(2,1)S(1)} fusion(bf16[16,128,2,128]{3,2,1,0:T(2,128)(2,1)S(1)} %reshape.87, bf16[2,4,128]{2,1,0:T(4,128)(2,1)S(1)} %convert_element_type.24, s32[2,4]{1,0:T(2,128)S(1)} %add_bitcast_fusion), kind=kOutput, calls=%fused_computation.5 | convolution fusion | flops 4456576 | bytes 1312800 | tf_op jit(solution)/shard_map/jqmr,rajc->jqmac/dot_general | solution.py:65
  88.5 0.7 copy.29
  (4 shorter events, 0.0 us)
Async XLA Ops:
  6.5 55.0 %all-gather.3.cloned.1.call-start = ((), (), s32[]{:S(2)}) async-start(), calls=%async_computation | async-start | bytes 2359296 | tf_op jit(solution)/shard_map/all_gather | solution.py:39
  9.0 77.0 %all-gather.5.cloned.1.call-start = ((), (), s32[]{:S(2)}) async-start(), calls=%async_computation.1 | async-start | bytes 1310720 | tf_op jit(solution)/shard_map/all_gather | solution.py:55
  61.5 8.8 %copy-start.1 = (s32[2,1,4]{2,1,0:T(1,128)S(1)}, s32[2,1,4]{2,1,0:T(1,128)}, u32[]{:S(2)}) copy-start(s32[2,1,4]{2,1,0:T(1,128)} %param.6) | copy-start | bytes 100
  61.5 14.1 %copy-start = (s32[2,4,128]{2,1,0:T(4,128)S(1)}, s32[2,4,128]{2,1,0:T(4,128)}, u32[]{:S(2)}) copy-start(s32[2,4,128]{2,1,0:T(4,128)} %param.7) | copy-start | bytes 12292
Sparse Core Ops, SparseCore 0:
  9.5 51.9 all-gather.2
  70.4 15.4 all-gather.4
where the time goes:
time: 96.4 us; the launch traced here: 96.1 us
  waiting for transfers between devices  49 us (51%)
  blocking collectives  23.3 us (24%)
  between operations  13.5 us (14%)
  matrix products  3.6 us (4%)
  other arithmetic  3.53 us (4%)
  local copies, waits for them, and re-layouts  3.11 us (3%)
    all_gather x1, waiting for transfers between devices, per_device(): dense_left = lax.all_gather(dense_own, 'blk', axis=0, tiled=True)  38.7 us
    all_gather x1, waiting for transfers between devices, per_device(): lax.all_gather(scaled, 'layer', axis=0, tiled=True)  10.3 us
    all_gather x1, blocking collectives, per_device(): lax.all_gather(tile_values, 'layer', axis=1, tiled=True)  6.42 us
    all_gather x1, blocking collectives, per_device(): lax.all_gather(band_rows, 'layer', axis=1, tiled=True)  6.18 us
    psum x1, blocking collectives, per_device(): totals = lax.psum(partial_value, 'layer')  5.67 us
    all_gather x1, blocking collectives, per_device(): lax.all_gather(kept_rows, 'layer', axis=1, tiled=True)  5.07 us
    dot_general x1, matrix products, per_device(): lax.dot_general(left_blocks, operand, (((0, 2), (0, 1)), ((), ())), prefe...  2.37 us
  transfers between devices with their start and end apart: 2, of which 2 were waited for; matrix products, arithmetic and copies ran while one was open for 1% of the time, Pallas kernels for 0%

commit v1 on v0

v1 whole, which is shorter than its diff:
```python
import functools

import jax
import jax.numpy as jnp
from jax import lax
from jax.experimental import pallas as pl
from jax.experimental.pallas import tpu as pltpu
from jax.sharding import PartitionSpec as P

MESH = pl.DeviceIdType.MESH
NOTE = 16


def each(count, body, most=8):
    if count <= most:
        for i in range(count):
            body(i)
    else:
        lax.fori_loop(0, count, lambda i, carry: (body(i), carry)[1], 0)


def kernel(
    cycle, bands, tiles_ref, rows_ref, kept_ref, mask_ref, out_ref,
    left, right, expanded, totals, stage,
    line_send, pair_send, layer_send, left_recv, right_recv,
    total_send, total_recv, out_send, out_recv,
):
    panels, per_band, tile = tiles_ref.shape[0], tiles_ref.shape[2], tiles_ref.shape[3]
    per_layer = out_ref.shape[2]
    count = panels * per_band
    body = count * tile
    band_blocks = panels * cycle // bands
    owners = band_blocks // panels
    me, layer = lax.axis_index("blk"), lax.axis_index("layer")
    half = cycle // 2
    pair = me + 1 - 2 * lax.rem(me, 2)
    line = [lax.rem(me + 2 * s, cycle) for s in range(1, half)]
    sources = [lax.rem(me + cycle - 2 * s, cycle) for s in range(1, half)]
    others = [lax.rem(layer + s, bands) for s in range(1, bands)]
    other_sources = [lax.rem(layer + bands - s, bands) for s in range(1, bands)]

    barrier = pltpu.get_barrier_semaphore()
    for peer in line + [pair]:
        pl.semaphore_signal(barrier, inc=1, device_id={"blk": peer}, device_id_type=MESH)
    for peer in others:
        pl.semaphore_signal(barrier, inc=1, device_id={"layer": peer}, device_id_type=MESH)

    row_ids = lax.broadcasted_iota(jnp.int32, (NOTE, tile), 0)
    note = jnp.zeros((NOTE, tile), jnp.float32)
    for j in range(panels):
        for k in range(per_band):
            at = j * per_band + k
            left[me, at * tile:(at + 1) * tile, :] = tiles_ref[j, 0, k]
            note = jnp.where(row_ids == at, rows_ref[j, 0, k].astype(jnp.float32), note)
    left[me, body:body + NOTE, :] = note.astype(jnp.bfloat16)

    pl.semaphore_wait(barrier, len(line) + 1 + len(others))

    def send_left(slot, target, send_sem):
        return pltpu.make_async_remote_copy(
            src_ref=left.at[slot], dst_ref=left.at[slot], send_sem=send_sem,
            recv_sem=left_recv.at[slot], device_id={"blk": target}, device_id_type=MESH,
        )

    copies = []
    for s, peer in enumerate(line):
        copies.append(send_left(me, peer, line_send.at[s]))
    copies.append(send_left(me, pair, pair_send.at[0]))
    for s, peer in enumerate(others):
        copies.append(pltpu.make_async_remote_copy(
            src_ref=left.at[me], dst_ref=right.at[layer], send_sem=layer_send.at[s],
            recv_sem=right_recv.at[layer], device_id={"layer": peer}, device_id_type=MESH,
        ))
    for copy in copies:
        copy.start()
    right[layer] = left[me]

    for s, source in enumerate(sources):
        send_left(source, pair, pair_send.at[0]).wait_recv()
        onward = send_left(source, pair, pair_send.at[s + 1])
        onward.start()
        copies.append(onward)
    send_left(pair, pair, pair_send.at[0]).wait_recv()
    for source in sources:
        twin = source + 1 - 2 * lax.rem(source, 2)
        send_left(twin, pair, pair_send.at[0]).wait_recv()
    for source in other_sources:
        pltpu.make_async_remote_copy(
            src_ref=left.at[me], dst_ref=right.at[source], send_sem=layer_send.at[0],
            recv_sem=right_recv.at[source], device_id={"layer": others[0]}, device_id_type=MESH,
        ).wait_recv()

    for p in range(panels):
        for b in range(band_blocks):
            expanded[p, b] = jnp.zeros((tile, tile), jnp.float32)

        def product(q, p=p):
            wanted = right[q, body:body + NOTE, :].astype(jnp.float32)
            for k in range(per_band):
                at = p * per_band + k
                want = wanted[at:at + 1]
                factor = right[q, at * tile:(at + 1) * tile, :]
                for kk in range(per_band):

                    def choose(o, carry):
                        block, landing = carry
                        owner = q * owners + o
                        notes = left[owner, body:body + NOTE, :].astype(jnp.float32)
                        for j in range(panels):
                            t = j * per_band + kk
                            r = jnp.asarray(o * panels + j).astype(jnp.float32)
                            pick = jnp.where(want == r, 1.0, 0.0)
                            block = block + left[owner, t * tile:(t + 1) * tile, :] * pick.astype(jnp.bfloat16)
                            landing = landing + notes[t:t + 1] * pick
                        return block, landing

                    carry = jnp.zeros((tile, tile), jnp.bfloat16), jnp.zeros((1, tile), jnp.float32)
                    if owners <= 4:
                        for o in range(owners):
                            carry = choose(o, carry)
                    else:
                        carry = lax.fori_loop(0, owners, choose, carry)
                    block, landing = carry
                    term = jnp.dot(block, factor, preferred_element_type=jnp.float32)

                    def land(b):
                        here = landing == jnp.asarray(b).astype(jnp.float32)
                        expanded[p, b] += jnp.where(here, term, 0.0)

                    each(band_blocks, land, 4)

        each(bands, product, 4 if per_band == 1 else 0)

        partial = jnp.zeros((1, tile), jnp.float32)
        for b in range(band_blocks):
            values = expanded[p, b]
            partial = partial + jnp.sum(values * values, axis=0, keepdims=True)
        totals[layer, p] = jnp.broadcast_to(partial, (8, tile))

    def send_total(s, peer, slot):
        return pltpu.make_async_remote_copy(
            src_ref=totals.at[slot], dst_ref=totals.at[slot], send_sem=total_send.at[s],
            recv_sem=total_recv.at[slot], device_id={"layer": peer}, device_id_type=MESH,
        )

    for s, peer in enumerate(others):
        copy = send_total(s, peer, layer)
        copy.start()
        copies.append(copy)
    for source in other_sources:
        send_total(0, others[0], source).wait_recv()

    row_count = float(panels * cycle * tile)
    factors = []
    for p in range(panels):
        total = totals[0, p]
        for q in range(1, bands):
            total = total + totals[q, p]
        keep = mask_ref[p, pl.ds(layer, 1), :].astype(jnp.float32)
        factors.append((row_count / total[0:1], keep))

    def block_of(p, m, j):
        scale, keep = factors[p]
        values = expanded[p, kept_ref[p, 0, m * per_layer + j]]
        return (values * values * scale * keep).astype(jnp.bfloat16)

    def send_out(s, peer, band):
        return pltpu.make_async_remote_copy(
            src_ref=stage.at[s], dst_ref=out_ref.at[:, band], send_sem=out_send.at[s],
            recv_sem=out_recv.at[band], device_id={"layer": peer}, device_id_type=MESH,
        )

    for s, peer in enumerate(others):
        for p in range(panels):
            for j in range(per_layer):
                stage[s, p, j] = block_of(p, peer, j)
        copy = send_out(s, peer, layer)
        copy.start()
        copies.append(copy)
    for p in range(panels):
        for j in range(per_layer):
            out_ref[p, layer, j] = block_of(p, layer, j)
    for source in other_sources:
        send_out(0, others[0], source).wait_recv()
    for copy in copies:
        copy.wait_send()


def solution(mesh):
    cycle, bands = mesh.shape["blk"], mesh.shape["layer"]

    def per_device(tile_values, band_rows, kept_rows, prune_mask):
        panels, _, per_band, tile, _ = tile_values.shape
        per_layer = kept_rows.shape[2] // bands
        band_blocks = panels * cycle // bands
        message = panels * per_band * tile + NOTE
        dma = pltpu.SemaphoreType.DMA
        vmem = pl.BlockSpec(memory_space=pltpu.VMEM)
        smem = pl.BlockSpec(memory_space=pltpu.SMEM)
        return pl.pallas_call(
            functools.partial(kernel, cycle, bands),
            out_shape=jax.ShapeDtypeStruct((panels, bands, per_layer, tile, tile), jnp.bfloat16),
            in_specs=[vmem, smem, smem, vmem],
            out_specs=vmem,
            scratch_shapes=[
                pltpu.VMEM((cycle, message, tile), jnp.bfloat16),
                pltpu.VMEM((bands, message, tile), jnp.bfloat16),
                pltpu.VMEM((panels, band_blocks, tile, tile), jnp.float32),
                pltpu.VMEM((bands, panels, 8, tile), jnp.float32),
                pltpu.VMEM((bands - 1, panels, per_layer, tile, tile), jnp.bfloat16),
                dma((cycle // 2,)),
                dma((cycle // 2,)),
                dma((bands,)),
                dma((cycle,)),
                dma((bands,)),
                dma((bands,)),
                dma((bands,)),
                dma((bands,)),
                dma((bands,)),
            ],
            compiler_params=pltpu.CompilerParams(
                collective_id=0, has_side_effects=True, vmem_limit_bytes=32 * 1024 * 1024
            ),
        )(tile_values, band_rows, kept_rows, prune_mask)

    return jax.shard_map(
        per_device,
        mesh=mesh,
        in_specs=(
            P("blk", "layer", None, None, None),
            P("blk", "layer", None),
            P("blk", "layer", None),
            P("blk", None, None),
        ),
        out_specs=P("blk", None, "layer", None, None),
        check_vma=False,
    )
```

time: 96.4 us -> 27.5 us (0.29)
  waiting for transfers between devices: 49 us -> 0 us
  Pallas kernels: 0 us -> 24.1 us
  blocking collectives: 23.3 us -> 0 us
  between operations: 13.5 us -> 0.01 us
  matrix products: 3.6 us -> 0 us
  other arithmetic: 3.53 us -> 0 us
    all_gather x2 -> x0, waiting for transfers between devices: 49 us -> none  [the longest x1 38.7 us: per_device(): dense_left = lax.all_gather(dense_own, 'blk', axis=0, tiled=True)]
    pallas_call x0 -> x1, Pallas kernels: none -> 24.1 us  [per_device(): pl.pallas_call(functools.partial(kernel, cycle, bands), out_shape=jax.Sha...]
    all_gather x3 -> x0, blocking collectives: 17.7 us -> none  [the longest x1 6.42 us: per_device(): lax.all_gather(tile_values, 'layer', axis=1, tiled=True)]
    psum x1 -> x0, blocking collectives: 5.67 us -> none  [per_device(): totals = lax.psum(partial_value, 'layer')]
    dot_general x2 -> x0, matrix products: 3.6 us -> none  [the longest x1 2.37 us: per_device(): lax.dot_general(left_blocks, operand, (((0, 2), (0, 1)), ((), ())), prefe...]
    unnamed x5 -> x8, local copies, waits for them, and re-layouts: 0.11 us -> 2.99 us
    convert_element_type x4 -> x0, other arithmetic: 1.81 us -> none  [the longest x2 1.06 us: densify(): return dense.astype(jnp.bfloat16)]
    another operation x4 -> x0, other arithmetic: 1.7 us -> none
  transfers between devices with their start and end apart: 2 -> 0, of which waited for: 2 -> 0; matrix products, arithmetic and copies ran while one was open for 1% -> 0% of each run, Pallas kernels for 0% -> 0%
where the time goes in v1:
time: 27.5 us; the launch traced here: 27.1 us
  Pallas kernels  24.1 us (88%)
  local copies, waits for them, and re-layouts  2.99 us (11%)
    pallas_call x1, Pallas kernels, per_device(): pl.pallas_call(functools.partial(kernel, cycle, bands), out_shape=jax.Sha...  24.1 us
    unnamed x8, local copies, waits for them, and re-layouts  2.99 us

profile of v1, /device:TPU:0, one launch (start us, length us, event | category | flops | bytes accessed | tf_op | source)
XLA Modules:
  0.0 27.1 jit_solution(13802561767066844708)
XLA Ops:
  0.0 0.0 copy-start.2
  0.0 0.8 %copy.5.rows_ref = s32[2,1,1]{2,1,0:T(1,128)S(1)} copy(s32[2,1,1]{0,2,1:T(1,128)} %param.5) | data formatting | bytes 16 | tf_op args[1]
  0.8 0.0 copy-done.2
  0.8 0.0 copy-start
  0.8 0.8 %copy-done = bf16[2,1,1,128,128]{4,3,2,1,0:T(8,128)(2,1)S(1)} copy-done((bf16[2,1,1,128,128]{4,3,2,1,0:T(8,128)(2,1)S(1)}, bf16[2,1,1,128,128]{4,3,2,1,0:T(8,128)(2,1)}, u32[]{:S(2)}) %copy-start) | copy-done | bytes 65560
  1.6 0.0 copy-start.1
  1.6 0.7 %copy-done.1 = s32[2,4,128]{2,1,0:T(4,128)S(1)} copy-done((s32[2,4,128]{2,1,0:T(4,128)S(1)}, s32[2,4,128]{2,1,0:T(4,128)}, u32[]{:S(2)}) %copy-start.1) | copy-done | bytes 4120
  2.3 24.1 %shard_map.46 = bf16[2,4,1,128,128]{4,3,2,1,0:T(8,128)(2,1)S(1)} custom-call(bf16[2,1,1,128,128]{4,3,2,1,0:T(8,128)(2,1)S(1)} %copy-done, s32[2,1,1]{2,1,0:T(1,128)S(1)} %copy.5.rows_ref, s32[2,1,4]{2,1,0:T(1,128)S(1)} %copy-done.2, s32[2,4,128]{2,1,0:T(4,128)S(1)} %copy-done.1), custom_call_target="tpu_custom_call" | custom-call | tf_op jit(solution)/shard_map/pallas_call | solution.py:200
  26.4 0.7 %copy.7 = bf16[2,4,1,128,128]{4,3,2,1,0:T(8,128)(2,1)} copy(bf16[2,4,1,128,128]{4,3,2,1,0:T(8,128)(2,1)S(1)} %shard_map.46) | data formatting | bytes 524288
Async XLA Ops:
  0.0 0.8 %copy-start.2 = (s32[2,1,4]{2,1,0:T(1,128)S(1)}, s32[2,1,4]{2,1,0:T(1,128)}, u32[]{:S(2)}) copy-start(s32[2,1,4]{2,1,0:T(1,128)} %kept_ref.1) | copy-start | bytes 100
  0.8 0.8 %copy-start = (bf16[2,1,1,128,128]{4,3,2,1,0:T(8,128)(2,1)S(1)}, bf16[2,1,1,128,128]{4,3,2,1,0:T(8,128)(2,1)}, u32[]{:S(2)}) copy-start(bf16[2,1,1,128,128]{4,3,2,1,0:T(8,128)(2,1)} %tiles_ref.1) | copy-start | bytes 196612
  1.6 0.7 %copy-start.1 = (s32[2,4,128]{2,1,0:T(4,128)S(1)}, s32[2,4,128]{2,1,0:T(4,128)}, u32[]{:S(2)}) copy-start(s32[2,4,128]{2,1,0:T(4,128)} %mask_ref.1) | copy-start | bytes 12292

commit v2 on v1

v2 whole, which is shorter than its diff:
```python
import functools

import jax
import jax.numpy as jnp
from jax import lax
from jax.experimental import pallas as pl
from jax.experimental.pallas import tpu as pltpu
from jax.sharding import PartitionSpec as P

MESH = pl.DeviceIdType.MESH
NOTE = 16


def each(count, body, most=8):
    if count <= most:
        for i in range(count):
            body(i)
    else:
        lax.fori_loop(0, count, lambda i, carry: (body(i), carry)[1], 0)


def xor(a, c):
    result, bit = a, 1
    while bit <= c:
        if c // bit % 2:
            result = result + bit * (1 - 2 * lax.rem(a // bit, 2))
        bit *= 2
    return result


def kernel(
    cycle, bands, panels, per_band, tiles_hbm, rows_hbm, kept_hbm, mask_hbm, out_ref,
    left, right, expanded, totals, stage, rows_ref, kept_ref, mask_ref,
    local, line_send, pair_send, layer_send, left_recv, right_recv,
    total_send, total_recv, out_send, out_recv, keep_sem,
):
    tile = tiles_hbm.shape[1]
    per_layer = out_ref.shape[2]
    count = panels * per_band
    body = count * tile
    band_blocks = panels * cycle // bands
    owners = band_blocks // panels
    lanes = owners // 2
    me, layer = lax.axis_index("blk"), lax.axis_index("layer")
    side = lax.rem(me, 2)
    pair = me + 1 - 2 * side
    mine = me // 2
    own_band, own_lane = mine // lanes, lax.rem(mine, lanes)
    others = [lax.rem(layer + s, bands) for s in range(1, bands)]

    def owners_of(d, which):
        band = xor(own_band, d)
        return [2 * (band * lanes + lax.rem(own_lane + h, lanes)) + which for h in range(lanes)]

    line = [owners_of(d, side) for d in range(bands)]
    line[0] = line[0][1:]
    targets = []
    for d in range(bands):
        band = xor(own_band, d)
        for h in range(lanes):
            if d or h:
                targets.append(2 * (band * lanes + lax.rem(own_lane + lanes - h, lanes)) + side)

    fetch_rows = pltpu.make_async_copy(rows_hbm, rows_ref, local.at[0])
    fetch_tiles = pltpu.make_async_copy(tiles_hbm, left.at[me, pl.ds(0, body)], local.at[1])
    fetch_right = pltpu.make_async_copy(tiles_hbm, right.at[layer, pl.ds(0, body)], local.at[2])
    fetch_kept = pltpu.make_async_copy(kept_hbm, kept_ref, local.at[3])
    fetch_mask = pltpu.make_async_copy(mask_hbm, mask_ref, local.at[4])
    for fetch in (fetch_rows, fetch_tiles, fetch_right, fetch_kept, fetch_mask):
        fetch.start()

    barrier = pltpu.get_barrier_semaphore()
    for peer in targets + [pair]:
        pl.semaphore_signal(barrier, inc=1, device_id={"blk": peer}, device_id_type=MESH)
    for peer in others:
        pl.semaphore_signal(barrier, inc=1, device_id={"layer": peer}, device_id_type=MESH)

    fetch_rows.wait()
    row_ids = lax.broadcasted_iota(jnp.int32, (NOTE, tile), 0)
    note = jnp.zeros((NOTE, tile), jnp.float32)
    for j in range(panels):
        for k in range(per_band):
            note = jnp.where(row_ids == j * per_band + k, rows_ref[0, k, j].astype(jnp.float32), note)
    note = note.astype(jnp.bfloat16)
    left[me, body:body + NOTE, :] = note
    right[layer, body:body + NOTE, :] = note
    fetch_tiles.wait()

    pl.semaphore_wait(barrier, len(targets) + 1 + len(others))

    def send_left(slot, target, send_sem):
        return pltpu.make_async_remote_copy(
            src_ref=left.at[slot], dst_ref=left.at[slot], send_sem=send_sem,
            recv_sem=left_recv.at[slot], device_id={"blk": target}, device_id_type=MESH,
        )

    def send_right(s, peer, band):
        return pltpu.make_async_remote_copy(
            src_ref=left.at[me], dst_ref=right.at[band], send_sem=layer_send.at[s],
            recv_sem=right_recv.at[band], device_id={"layer": peer}, device_id_type=MESH,
        )

    copies = [send_left(me, pair, pair_send.at[0])]
    for s, peer in enumerate(targets):
        copies.append(send_left(me, peer, line_send.at[s]))
    for s, peer in enumerate(others):
        copies.append(send_right(s, peer, layer))
    for copy in copies:
        copy.start()

    def forward(d):
        for source in line[d]:
            send_left(source, pair, pair_send.at[0]).wait_recv()
            onward = send_left(source, pair, pair_send.at[len(copies) - len(targets) - len(others)])
            onward.start()
            copies.append(onward)

    def product(d, p):
        q = xor(own_band, d)
        wanted = right[q, body:body + NOTE, :].astype(jnp.float32)
        for k in range(per_band):
            at = p * per_band + k
            want = wanted[at:at + 1]
            factor = right[q, at * tile:(at + 1) * tile, :]
            for kk in range(per_band):

                def choose(o, carry):
                    block, landing = carry
                    owner = q * owners + o
                    notes = left[owner, body:body + NOTE, :].astype(jnp.float32)
                    for j in range(panels):
                        t = j * per_band + kk
                        r = jnp.asarray(o * panels + j).astype(jnp.float32)
                        pick = jnp.where(want == r, 1.0, 0.0)
                        block = block + left[owner, t * tile:(t + 1) * tile, :] * pick.astype(jnp.bfloat16)
                        landing = landing + notes[t:t + 1] * pick
                    return block, landing

                carry = jnp.zeros((tile, tile), jnp.bfloat16), jnp.zeros((1, tile), jnp.float32)
                if owners <= 4:
                    for o in range(owners):
                        carry = choose(o, carry)
                else:
                    carry = lax.fori_loop(0, owners, choose, carry)
                block, landing = carry
                term = jnp.dot(block, factor, preferred_element_type=jnp.float32)

                def land(b):
                    here = landing == jnp.asarray(b).astype(jnp.float32)
                    value = jnp.where(here, term, 0.0)
                    if d or k or kk:
                        value = expanded[p, b] + value
                    expanded[p, b] = value

                each(band_blocks, land, 4)

    def arrive(d):
        for twin in owners_of(d, 1 - side):
            send_left(twin, pair, pair_send.at[0]).wait_recv()

    def send_total(s, peer, slot, p):
        return pltpu.make_async_remote_copy(
            src_ref=totals.at[slot, p], dst_ref=totals.at[slot, p], send_sem=total_send.at[s, p],
            recv_sem=total_recv.at[slot, p], device_id={"layer": peer}, device_id_type=MESH,
        )

    forward(0)
    forward(1)
    fetch_right.wait()
    for s, peer in enumerate(others):
        send_right(s, peer, peer).wait_recv()
    for d in range(bands):
        arrive(d)
        last = d == bands - 1
        for p in range(panels):
            product(d, p)
            if last:
                partial = jnp.zeros((1, tile), jnp.float32)
                for b in range(band_blocks):
                    values = expanded[p, b]
                    partial = partial + jnp.sum(values * values, axis=0, keepdims=True)
                totals[layer, p] = jnp.broadcast_to(partial, (8, tile))
                for s, peer in enumerate(others):
                    copy = send_total(s, peer, layer, p)
                    copy.start()
                    copies.append(copy)
        if d + 2 < bands:
            forward(d + 2)

    row_count = float(panels * cycle * tile)
    fetch_kept.wait()
    fetch_mask.wait()

    def send_out(s, peer, band, p):
        return pltpu.make_async_remote_copy(
            src_ref=stage.at[s, p], dst_ref=out_ref.at[p, band], send_sem=out_send.at[s, p],
            recv_sem=out_recv.at[band, p], device_id={"layer": peer}, device_id_type=MESH,
        )

    keeps = []
    for p in range(panels):
        for s, source in enumerate(others):
            send_total(s, source, source, p).wait_recv()
        total = totals[0, p]
        for q in range(1, bands):
            total = total + totals[q, p]
        scale = row_count / total[0:1]
        keep = mask_ref[p, pl.ds(layer, 1), :].astype(jnp.float32)

        def block_of(m, j):
            values = expanded[p, kept_ref[p, 0, m * per_layer + j]]
            return (values * values * scale * keep).astype(jnp.bfloat16)

        for s, peer in enumerate(others):
            for j in range(per_layer):
                stage[s, p, j] = block_of(peer, j)
            copy = send_out(s, peer, layer, p)
            copy.start()
            copies.append(copy)
        for j in range(per_layer):
            stage[bands - 1, p, j] = block_of(layer, j)
        keeps.append(pltpu.make_async_copy(stage.at[bands - 1, p], out_ref.at[p, layer], keep_sem.at[p]))
        keeps[-1].start()
    for p in range(panels):
        for s, source in enumerate(others):
            send_out(s, source, source, p).wait_recv()
    for copy in keeps:
        copy.wait()
    for copy in copies:
        copy.wait_send()


def solution(mesh):
    cycle, bands = mesh.shape["blk"], mesh.shape["layer"]

    def per_device(tile_values, band_rows, kept_rows, prune_mask):
        panels, _, per_band, tile, _ = tile_values.shape
        per_layer = kept_rows.shape[2] // bands
        band_blocks = panels * cycle // bands
        message = panels * per_band * tile + NOTE
        dma = pltpu.SemaphoreType.DMA
        hbm = pl.BlockSpec(memory_space=pltpu.HBM)
        return pl.pallas_call(
            functools.partial(kernel, cycle, bands, panels, per_band),
            out_shape=jax.ShapeDtypeStruct((panels, bands, per_layer, tile, tile), jnp.bfloat16),
            in_specs=[hbm] * 4,
            out_specs=hbm,
            scratch_shapes=[
                pltpu.VMEM((cycle, message, tile), jnp.bfloat16),
                pltpu.VMEM((bands, message, tile), jnp.bfloat16),
                pltpu.VMEM((panels, band_blocks, tile, tile), jnp.float32),
                pltpu.VMEM((bands, panels, 8, tile), jnp.float32),
                pltpu.VMEM((bands, panels, per_layer, tile, tile), jnp.bfloat16),
                pltpu.SMEM((1, per_band, panels), jnp.int32),
                pltpu.SMEM(kept_rows.shape, jnp.int32),
                pltpu.VMEM(prune_mask.shape, jnp.int32),
                dma((5,)),
                dma((cycle // 2,)),
                dma((cycle // 2,)),
                dma((bands,)),
                dma((cycle,)),
                dma((bands,)),
                dma((bands, panels)),
                dma((bands, panels)),
                dma((bands, panels)),
                dma((bands, panels)),
                dma((panels,)),
            ],
            compiler_params=pltpu.CompilerParams(
                collective_id=0, has_side_effects=True, vmem_limit_bytes=63 * 1024 * 1024
            ),
        )(
            tile_values.reshape(panels * per_band * tile, tile),
            band_rows.transpose(1, 2, 0),
            kept_rows,
            prune_mask,
        )

    return jax.shard_map(
        per_device,
        mesh=mesh,
        in_specs=(
            P("blk", "layer", None, None, None),
            P("blk", "layer", None),
            P("blk", "layer", None),
            P("blk", None, None),
        ),
        out_specs=P("blk", None, "layer", None, None),
        check_vma=False,
    )
```

time: 27.5 us -> 26 us (0.945)
  local copies, waits for them, and re-layouts: 2.99 us -> 1.67 us
    unnamed x8 -> x1, local copies, waits for them, and re-layouts: 2.99 us -> 1.67 us
where the time goes in v2:
time: 26 us; the launch traced here: 25.9 us
  Pallas kernels  24.2 us (93%)
  local copies, waits for them, and re-layouts  1.67 us (6%)
    pallas_call x1, Pallas kernels, per_device(): pl.pallas_call(functools.partial(kernel, cycle, bands, panels, per_band),...  24.2 us
    unnamed x1, local copies, waits for them, and re-layouts  1.67 us

profile of v2, /device:TPU:0, one launch (start us, length us, event | category | flops | bytes accessed | tf_op | source)
XLA Modules:
  0.0 25.9 jit_solution(16918130398102837408)
XLA Ops:
  0.0 24.2 %shard_map.46 = bf16[2,4,1,128,128]{4,3,2,1,0:T(8,128)(2,1)} custom-call(bf16[256,128]{1,0:T(8,128)(2,1)} %bitcast.2, s32[1,1,2]{2,1,0:T(1,128)} %bitcast.3, s32[2,1,4]{2,1,0:T(1,128)} %kept_hbm.1, s32[2,4,128]{2,1,0:T(4,128)} %mask_hbm.1), custom_call_target="tpu_custom_call" | custom-call | tf_op jit(solution)/shard_map/pallas_call | solution.py:243
  24.2 1.7 %copy.6 = bf16[2,4,1,128,128]{4,3,2,1,0:T(8,128)(2,1)} copy(bf16[2,4,1,128,128]{4,3,2,1,0:T(8,128)(2,1)} %shard_map.46) | data formatting | bytes 524288

commit v3 on v2

--- a/solution.py
+++ b/solution.py
@@ -62,8 +62,8 @@
                 targets.append(2 * (band * lanes + lax.rem(own_lane + lanes - h, lanes)) + side)
 
     fetch_rows = pltpu.make_async_copy(rows_hbm, rows_ref, local.at[0])
-    fetch_tiles = pltpu.make_async_copy(tiles_hbm, left.at[me, pl.ds(0, body)], local.at[1])
-    fetch_right = pltpu.make_async_copy(tiles_hbm, right.at[layer, pl.ds(0, body)], local.at[2])
+    fetch_tiles = pltpu.make_async_copy(tiles_hbm, left.at[me, pl.ds(NOTE, body)], local.at[1])
+    fetch_right = pltpu.make_async_copy(tiles_hbm, right.at[layer, pl.ds(NOTE, body)], local.at[2])
     fetch_kept = pltpu.make_async_copy(kept_hbm, kept_ref, local.at[3])
     fetch_mask = pltpu.make_async_copy(mask_hbm, mask_ref, local.at[4])
     for fetch in (fetch_rows, fetch_tiles, fetch_right, fetch_kept, fetch_mask):
@@ -82,16 +82,20 @@
         for k in range(per_band):
             note = jnp.where(row_ids == j * per_band + k, rows_ref[0, k, j].astype(jnp.float32), note)
     note = note.astype(jnp.bfloat16)
-    left[me, body:body + NOTE, :] = note
-    right[layer, body:body + NOTE, :] = note
+    left[me, 0:NOTE, :] = note
+    right[layer, 0:NOTE, :] = note
     fetch_tiles.wait()
 
     pl.semaphore_wait(barrier, len(targets) + 1 + len(others))
 
-    def send_left(slot, target, send_sem):
-        return pltpu.make_async_remote_copy(
-            src_ref=left.at[slot], dst_ref=left.at[slot], send_sem=send_sem,
-            recv_sem=left_recv.at[slot], device_id={"blk": target}, device_id_type=MESH,
+    part = per_band * tile
+    chunks = [(NOTE + c * part if c else 0, part if c else NOTE + part) for c in range(panels)]
+
+    def send_left(slot, target, send_sem, c):
+        rows = pl.ds(*chunks[c])
+        return pltpu.make_async_remote_copy(
+            src_ref=left.at[slot, rows], dst_ref=left.at[slot, rows], send_sem=send_sem,
+            recv_sem=left_recv.at[slot, c], device_id={"blk": target}, device_id_type=MESH,
         )
 
     def send_right(s, peer, band):
@@ -100,39 +104,42 @@
             recv_sem=right_recv.at[band], device_id={"layer": peer}, device_id_type=MESH,
         )
 
-    copies = [send_left(me, pair, pair_send.at[0])]
-    for s, peer in enumerate(targets):
-        copies.append(send_left(me, peer, line_send.at[s]))
+    copies = []
+    for c in range(panels):
+        copies.append(send_left(me, pair, pair_send.at[0, c], c))
+        for s, peer in enumerate(targets):
+            copies.append(send_left(me, peer, line_send.at[s, c], c))
     for s, peer in enumerate(others):
         copies.append(send_right(s, peer, layer))
     for copy in copies:
         copy.start()
 
-    def forward(d):
-        for source in line[d]:
-            send_left(source, pair, pair_send.at[0]).wait_recv()
-            onward = send_left(source, pair, pair_send.at[len(copies) - len(targets) - len(others)])
+    sources = [source for band in line for source in band]
+    for c in range(panels):
+        for s, source in enumerate(sources):
+            onward = send_left(source, pair, pair_send.at[s + 1, c], c)
+            onward.wait_recv()
             onward.start()
             copies.append(onward)
 
     def product(d, p):
         q = xor(own_band, d)
-        wanted = right[q, body:body + NOTE, :].astype(jnp.float32)
+        wanted = right[q, 0:NOTE, :].astype(jnp.float32)
         for k in range(per_band):
             at = p * per_band + k
             want = wanted[at:at + 1]
-            factor = right[q, at * tile:(at + 1) * tile, :]
+            factor = right[q, NOTE + at * tile:NOTE + (at + 1) * tile, :]
             for kk in range(per_band):
 
                 def choose(o, carry):
                     block, landing = carry
                     owner = q * owners + o
-                    notes = left[owner, body:body + NOTE, :].astype(jnp.float32)
+                    notes = left[owner, 0:NOTE, :].astype(jnp.float32)
                     for j in range(panels):
                         t = j * per_band + kk
                         r = jnp.asarray(o * panels + j).astype(jnp.float32)
                         pick = jnp.where(want == r, 1.0, 0.0)
-                        block = block + left[owner, t * tile:(t + 1) * tile, :] * pick.astype(jnp.bfloat16)
+                        block = block + left[owner, NOTE + t * tile:NOTE + (t + 1) * tile, :] * pick.astype(jnp.bfloat16)
                         landing = landing + notes[t:t + 1] * pick
                     return block, landing
 
@@ -155,8 +162,9 @@
                 each(band_blocks, land, 4)
 
     def arrive(d):
-        for twin in owners_of(d, 1 - side):
-            send_left(twin, pair, pair_send.at[0]).wait_recv()
+        for c in range(panels):
+            for twin in owners_of(d, 1 - side):
+                send_left(twin, pair, pair_send.at[0, c], c).wait_recv()
 
     def send_total(s, peer, slot, p):
         return pltpu.make_async_remote_copy(
@@ -164,8 +172,6 @@
             recv_sem=total_recv.at[slot, p], device_id={"layer": peer}, device_id_type=MESH,
         )
 
-    forward(0)
-    forward(1)
     fetch_right.wait()
     for s, peer in enumerate(others):
         send_right(s, peer, peer).wait_recv()
@@ -184,8 +190,6 @@
                     copy = send_total(s, peer, layer, p)
                     copy.start()
                     copies.append(copy)
-        if d + 2 < bands:
-            forward(d + 2)
 
     row_count = float(panels * cycle * tile)
     fetch_kept.wait()
@@ -255,10 +259,10 @@
                 pltpu.SMEM(kept_rows.shape, jnp.int32),
                 pltpu.VMEM(prune_mask.shape, jnp.int32),
                 dma((5,)),
-                dma((cycle // 2,)),
-                dma((cycle // 2,)),
+                dma((cycle // 2, panels)),
+                dma((cycle // 2, panels)),
                 dma((bands,)),
-                dma((cycle,)),
+                dma((cycle, panels)),
                 dma((bands,)),
                 dma((bands, panels)),
                 dma((bands, panels)),

time: 26 us -> 25.9 us (level)
  no operation moved by 1% of the time
where the time goes in v3:
time: 25.9 us; the launch traced here: 25.7 us
  Pallas kernels  24 us (93%)
  local copies, waits for them, and re-layouts  1.67 us (6%)
    pallas_call x1, Pallas kernels, per_device(): pl.pallas_call(functools.partial(kernel, cycle, bands, panels, per_band),...  24 us
    unnamed x1, local copies, waits for them, and re-layouts  1.67 us

profile of v3, /device:TPU:0, one launch (start us, length us, event | category | flops | bytes accessed | tf_op | source)
XLA Modules:
  0.0 25.7 jit_solution(16269734325078380885)
XLA Ops:
  0.0 24.0 %shard_map.46 = bf16[2,4,1,128,128]{4,3,2,1,0:T(8,128)(2,1)} custom-call(bf16[256,128]{1,0:T(8,128)(2,1)} %bitcast.2, s32[1,1,2]{2,1,0:T(1,128)} %bitcast.3, s32[2,1,4]{2,1,0:T(1,128)} %kept_hbm.1, s32[2,4,128]{2,1,0:T(4,128)} %mask_hbm.1), custom_call_target="tpu_custom_call" | custom-call | tf_op jit(solution)/shard_map/pallas_call | solution.py:247
  24.0 1.7 %copy.6 = bf16[2,4,1,128,128]{4,3,2,1,0:T(8,128)(2,1)} copy(bf16[2,4,1,128,128]{4,3,2,1,0:T(8,128)(2,1)} %shard_map.46) | data formatting | bytes 524288

commit v4 on v3

v4 whole, which is shorter than its diff:
```python
import functools

import jax
import jax.numpy as jnp
from jax import lax
from jax.experimental import pallas as pl
from jax.experimental.pallas import tpu as pltpu
from jax.sharding import PartitionSpec as P

MESH = pl.DeviceIdType.MESH
NOTE = 16


def each(count, body):
    lax.fori_loop(0, count, lambda i, carry: (body(i), carry)[1], 0)


def xor(a, c, count):
    result, bit = 0, 1
    while bit < count:
        result = result + bit * lax.rem(a // bit + c // bit, 2)
        bit *= 2
    return result


def kernel(
    cycle, bands, panels, per_band, tiles_hbm, rows_hbm, kept_hbm, mask_hbm, out_ref,
    left, right, expanded, totals, stage, rows_ref, kept_ref, mask_ref,
    local, line_send, pair_send, layer_send, left_recv, right_recv,
    total_send, total_recv, out_send, out_recv, keep_sem,
):
    tile = tiles_hbm.shape[1]
    per_layer = out_ref.shape[2]
    body = panels * per_band * tile
    band_blocks = panels * cycle // bands
    owners = band_blocks // panels
    lanes = owners // 2
    onward = cycle // 2 - 1
    me, layer = lax.axis_index("blk"), lax.axis_index("layer")
    side = lax.rem(me, 2)
    pair = me + 1 - 2 * side
    own_band, own_lane = me // owners, lax.rem(me // 2, lanes)

    def other(s):
        return lax.rem(layer + 1 + s, bands)

    def owner_at(i, which):
        band = xor(own_band, i // lanes, bands)
        return 2 * (band * lanes + lax.rem(own_lane + lax.rem(i, lanes), lanes)) + which

    def target_at(i):
        band = xor(own_band, i // lanes, bands)
        return 2 * (band * lanes + lax.rem(own_lane + lanes - lax.rem(i, lanes), lanes)) + side

    fetch_rows = pltpu.make_async_copy(rows_hbm, rows_ref, local.at[0])
    fetch_tiles = pltpu.make_async_copy(tiles_hbm, left.at[me, pl.ds(NOTE, body)], local.at[1])
    fetch_right = pltpu.make_async_copy(tiles_hbm, right.at[layer, pl.ds(NOTE, body)], local.at[2])
    fetch_kept = pltpu.make_async_copy(kept_hbm, kept_ref, local.at[3])
    fetch_mask = pltpu.make_async_copy(mask_hbm, mask_ref, local.at[4])

    barrier = pltpu.get_barrier_semaphore()

    def greet(peer):
        pl.semaphore_signal(barrier, inc=1, device_id=peer, device_id_type=MESH)

    greet({"blk": pair})
    each(onward, lambda i: greet({"blk": target_at(i + 1)}))
    each(bands - 1, lambda s: greet({"layer": other(s)}))
    for fetch in (fetch_rows, fetch_tiles, fetch_right, fetch_kept, fetch_mask):
        fetch.start()

    fetch_rows.wait()
    row_ids = lax.broadcasted_iota(jnp.int32, (NOTE, tile), 0)
    note = jnp.zeros((NOTE, tile), jnp.float32)
    for j in range(panels):
        for k in range(per_band):
            note = jnp.where(row_ids == j * per_band + k, rows_ref[0, k, j].astype(jnp.float32), note)
    note = note.astype(jnp.bfloat16)
    left[me, 0:NOTE, :] = note
    right[layer, 0:NOTE, :] = note
    fetch_tiles.wait()
    pl.semaphore_wait(barrier, onward + bands)

    part = per_band * tile
    chunks = [(NOTE + c * part if c else 0, part if c else NOTE + part) for c in range(panels)]

    def send_left(slot, target, send_sem, c):
        rows = pl.ds(*chunks[c])
        return pltpu.make_async_remote_copy(
            src_ref=left.at[slot, rows], dst_ref=left.at[slot, rows], send_sem=send_sem,
            recv_sem=left_recv.at[slot, c], device_id={"blk": target}, device_id_type=MESH,
        )

    def send_right(s, band):
        return pltpu.make_async_remote_copy(
            src_ref=left.at[me], dst_ref=right.at[band], send_sem=layer_send.at[s],
            recv_sem=right_recv.at[band], device_id={"layer": other(s)}, device_id_type=MESH,
        )

    def along(i, c):
        return send_left(me, target_at(i + 1), line_send.at[i, c], c)

    def across(i, c):
        return send_left(owner_at(i, side), pair, pair_send.at[i, c], c)

    for c in range(panels):
        across(0, c).start()
        each(onward, lambda i, c=c: along(i, c).start())
    each(bands - 1, lambda s: send_right(s, layer).start())

    def clear(i):
        for b in range(panels):
            expanded[b, i] = jnp.zeros((tile, tile), jnp.float32)

    each(band_blocks, clear)

    for c in range(panels):

        def forward(i, c=c):
            copy = across(i + 1, c)
            copy.wait_recv()
            copy.start()

        each(onward, forward)

    fetch_right.wait()
    each(bands - 1, lambda s: send_right(s, other(s)).wait_recv())

    def product(d):
        def arrive(h):
            for c in range(panels):
                send_left(owner_at(d * lanes + h, 1 - side), pair, pair_send.at[0, c], c).wait_recv()

        each(lanes, arrive)
        q = xor(own_band, d, bands)
        wanted = right[q, 0:NOTE, :].astype(jnp.float32)
        for p in range(panels):
            for k in range(per_band):
                at = p * per_band + k
                want = wanted[at:at + 1]
                factor = right[q, NOTE + at * tile:NOTE + (at + 1) * tile, :]
                for kk in range(per_band):

                    def choose(o, carry):
                        block, landing = carry
                        owner = q * owners + o
                        notes = left[owner, 0:NOTE, :].astype(jnp.float32)
                        for j in range(panels):
                            t = j * per_band + kk
                            r = jnp.asarray(o * panels + j).astype(jnp.float32)
                            pick = jnp.where(want == r, 1.0, 0.0)
                            tiles = left[owner, NOTE + t * tile:NOTE + (t + 1) * tile, :]
                            block = block + tiles * pick.astype(jnp.bfloat16)
                            landing = landing + notes[t:t + 1] * pick
                        return block, landing

                    carry = jnp.zeros((tile, tile), jnp.bfloat16), jnp.zeros((1, tile), jnp.float32)
                    if owners <= 4:
                        for o in range(owners):
                            carry = choose(o, carry)
                    else:
                        carry = lax.fori_loop(0, owners, choose, carry)
                    block, landing = carry
                    term = jnp.dot(block, factor, preferred_element_type=jnp.float32)

                    def land(b):
                        here = landing == jnp.asarray(b).astype(jnp.float32)
                        expanded[p, b] += jnp.where(here, term, 0.0)

                    if band_blocks <= 4:
                        for b in range(band_blocks):
                            land(b)
                    else:
                        each(band_blocks, land)

    each(bands, product)

    def send_total(s, slot):
        return pltpu.make_async_remote_copy(
            src_ref=totals.at[slot], dst_ref=totals.at[slot], send_sem=total_send.at[s],
            recv_sem=total_recv.at[slot], device_id={"layer": other(s)}, device_id_type=MESH,
        )

    def add(b, sums):
        values = [expanded[p, b] for p in range(panels)]
        return tuple(one + jnp.sum((v * v).reshape(tile // 8, 8, tile), axis=0) for one, v in zip(sums, values))

    sums = lax.fori_loop(0, band_blocks, add, (jnp.zeros((8, tile), jnp.float32),) * panels)
    for p in range(panels):
        totals[layer, p] = sums[p]
    each(bands - 1, lambda s: send_total(s, layer).start())

    row_count = float(panels * cycle * tile)
    fetch_kept.wait()
    fetch_mask.wait()

    def send_out(s, band, p):
        return pltpu.make_async_remote_copy(
            src_ref=stage.at[s, p], dst_ref=out_ref.at[p, band], send_sem=out_send.at[s, p],
            recv_sem=out_recv.at[band, p], device_id={"layer": other(s)}, device_id_type=MESH,
        )

    def keep_own(p):
        return pltpu.make_async_copy(stage.at[bands - 1, p], out_ref.at[p, layer], keep_sem.at[p])

    each(bands - 1, lambda s: send_total(s, other(s)).wait_recv())
    for p in range(panels):
        total = totals[0, p]
        for q in range(1, bands):
            total = total + totals[q, p]
        scale = row_count / jnp.sum(total, axis=0, keepdims=True)
        keep = mask_ref[p, pl.ds(layer, 1), :].astype(jnp.float32)

        def put(s, p=p, scale=scale, keep=keep):
            for j in range(per_layer):
                values = expanded[p, kept_ref[p, 0, other(s) * per_layer + j]]
                stage[s, p, j] = (values * values * scale * keep).astype(jnp.bfloat16)

        def ship(s, p=p, put=put):
            put(s)
            send_out(s, layer, p).start()

        each(bands - 1, ship)
        put(bands - 1)
        keep_own(p).start()

    for p in range(panels):
        each(bands - 1, lambda s, p=p: send_out(s, other(s), p).wait_recv())
        keep_own(p).wait()
    for c in range(panels):
        each(onward, lambda i, c=c: along(i, c).wait_send())
        each(onward + 1, lambda i, c=c: across(i, c).wait_send())
    each(bands - 1, lambda s: send_right(s, layer).wait_send())
    each(bands - 1, lambda s: send_total(s, layer).wait_send())
    for p in range(panels):
        each(bands - 1, lambda s, p=p: send_out(s, layer, p).wait_send())


def solution(mesh):
    cycle, bands = mesh.shape["blk"], mesh.shape["layer"]

    def per_device(tile_values, band_rows, kept_rows, prune_mask):
        panels, _, per_band, tile, _ = tile_values.shape
        per_layer = kept_rows.shape[2] // bands
        band_blocks = panels * cycle // bands
        message = panels * per_band * tile + NOTE
        dma = pltpu.SemaphoreType.DMA
        hbm = pl.BlockSpec(memory_space=pltpu.HBM)
        return pl.pallas_call(
            functools.partial(kernel, cycle, bands, panels, per_band),
            out_shape=jax.ShapeDtypeStruct((panels, bands, per_layer, tile, tile), jnp.bfloat16),
            in_specs=[hbm] * 4,
            out_specs=hbm,
            scratch_shapes=[
                pltpu.VMEM((cycle, message, tile), jnp.bfloat16),
                pltpu.VMEM((bands, message, tile), jnp.bfloat16),
                pltpu.VMEM((panels, band_blocks, tile, tile), jnp.float32),
                pltpu.VMEM((bands, panels, 8, tile), jnp.float32),
                pltpu.VMEM((bands, panels, per_layer, tile, tile), jnp.bfloat16),
                pltpu.SMEM((1, per_band, panels), jnp.int32),
                pltpu.SMEM(kept_rows.shape, jnp.int32),
                pltpu.VMEM(prune_mask.shape, jnp.int32),
                dma((5,)),
                dma((cycle // 2, panels)),
                dma((cycle // 2, panels)),
                dma((bands,)),
                dma((cycle, panels)),
                dma((bands,)),
                dma((bands,)),
                dma((bands,)),
                dma((bands, panels)),
                dma((bands, panels)),
                dma((panels,)),
            ],
            compiler_params=pltpu.CompilerParams(
                collective_id=0, has_side_effects=True, vmem_limit_bytes=63 * 1024 * 1024
            ),
        )(
            tile_values.reshape(panels * per_band * tile, tile),
            band_rows.transpose(1, 2, 0),
            kept_rows,
            prune_mask,
        )

    return jax.shard_map(
        per_device,
        mesh=mesh,
        in_specs=(
            P("blk", "layer", None, None, None),
            P("blk", "layer", None),
            P("blk", "layer", None),
            P("blk", None, None),
        ),
        out_specs=P("blk", None, "layer", None, None),
        check_vma=False,
    )
```

time: 25.9 us -> 26 us (level)
  no operation moved by 1% of the time
where the time goes in v4:
time: 26 us; the launch traced here: 25.8 us
  Pallas kernels  24.1 us (93%)
  local copies, waits for them, and re-layouts  1.67 us (6%)
    pallas_call x1, Pallas kernels, per_device(): pl.pallas_call(functools.partial(kernel, cycle, bands, panels, per_band),...  24.1 us
    unnamed x1, local copies, waits for them, and re-layouts  1.67 us

profile of v4, /device:TPU:0, one launch (start us, length us, event | category | flops | bytes accessed | tf_op | source)
XLA Modules:
  0.0 25.8 jit_solution(5583042333348374356)
XLA Ops:
  0.0 24.1 %shard_map.46 = bf16[2,4,1,128,128]{4,3,2,1,0:T(8,128)(2,1)} custom-call(bf16[256,128]{1,0:T(8,128)(2,1)} %bitcast.2, s32[1,1,2]{2,1,0:T(1,128)} %bitcast.3, s32[2,1,4]{2,1,0:T(1,128)} %kept_hbm.1, s32[2,4,128]{2,1,0:T(4,128)} %mask_hbm.1), custom_call_target="tpu_custom_call" | custom-call | tf_op jit(solution)/shard_map/pallas_call | solution.py:249
  24.2 1.7 %copy.6 = bf16[2,4,1,128,128]{4,3,2,1,0:T(8,128)(2,1)} copy(bf16[2,4,1,128,128]{4,3,2,1,0:T(8,128)(2,1)} %shard_map.46) | data formatting | bytes 524288

commit v5 on v4

--- a/solution.py
+++ b/solution.py
@@ -26,7 +26,7 @@
 def kernel(
     cycle, bands, panels, per_band, tiles_hbm, rows_hbm, kept_hbm, mask_hbm, out_ref,
     left, right, expanded, totals, stage, rows_ref, kept_ref, mask_ref,
-    local, line_send, pair_send, layer_send, left_recv, right_recv,
+    local, up_send, down_send, pair_send, layer_send, left_recv, right_recv,
     total_send, total_recv, out_send, out_recv, keep_sem,
 ):
     tile = tiles_hbm.shape[1]
@@ -35,10 +35,12 @@
     band_blocks = panels * cycle // bands
     owners = band_blocks // panels
     lanes = owners // 2
-    onward = cycle // 2 - 1
     me, layer = lax.axis_index("blk"), lax.axis_index("layer")
     side = lax.rem(me, 2)
     pair = me + 1 - 2 * side
+    half = cycle // 2
+    spot = me // 2
+    below, above = spot > 0, spot < half - 1
     own_band, own_lane = me // owners, lax.rem(me // 2, lanes)
 
     def other(s):
@@ -47,10 +49,6 @@
     def owner_at(i, which):
         band = xor(own_band, i // lanes, bands)
         return 2 * (band * lanes + lax.rem(own_lane + lax.rem(i, lanes), lanes)) + which
-
-    def target_at(i):
-        band = xor(own_band, i // lanes, bands)
-        return 2 * (band * lanes + lax.rem(own_lane + lanes - lax.rem(i, lanes), lanes)) + side
 
     fetch_rows = pltpu.make_async_copy(rows_hbm, rows_ref, local.at[0])
     fetch_tiles = pltpu.make_async_copy(tiles_hbm, left.at[me, pl.ds(NOTE, body)], local.at[1])
@@ -64,7 +62,8 @@
         pl.semaphore_signal(barrier, inc=1, device_id=peer, device_id_type=MESH)
 
     greet({"blk": pair})
-    each(onward, lambda i: greet({"blk": target_at(i + 1)}))
+    greet({"blk": lax.rem(me + 2, cycle)})
+    greet({"blk": lax.rem(me + cycle - 2, cycle)})
     each(bands - 1, lambda s: greet({"layer": other(s)}))
     for fetch in (fetch_rows, fetch_tiles, fetch_right, fetch_kept, fetch_mask):
         fetch.start()
@@ -79,7 +78,7 @@
     left[me, 0:NOTE, :] = note
     right[layer, 0:NOTE, :] = note
     fetch_tiles.wait()
-    pl.semaphore_wait(barrier, onward + bands)
+    pl.semaphore_wait(barrier, 2 + bands)
 
     part = per_band * tile
     chunks = [(NOTE + c * part if c else 0, part if c else NOTE + part) for c in range(panels)]
@@ -97,15 +96,19 @@
             recv_sem=right_recv.at[band], device_id={"layer": other(s)}, device_id_type=MESH,
         )
 
-    def along(i, c):
-        return send_left(me, target_at(i + 1), line_send.at[i, c], c)
-
-    def across(i, c):
-        return send_left(owner_at(i, side), pair, pair_send.at[i, c], c)
+    def up(t, c):
+        return send_left(me - 2 * t, me + 2, up_send.at[t, c], c)
+
+    def down(t, c):
+        return send_left(me + 2 * t, me - 2, down_send.at[t, c], c)
+
+    def across(place, c):
+        return send_left(2 * place + side, pair, pair_send.at[place, c], c)
 
     for c in range(panels):
-        across(0, c).start()
-        each(onward, lambda i, c=c: along(i, c).start())
+        pl.when(above)(lambda c=c: up(0, c).start())
+        pl.when(below)(lambda c=c: down(0, c).start())
+        across(spot, c).start()
     each(bands - 1, lambda s: send_right(s, layer).start())
 
     def clear(i):
@@ -114,14 +117,22 @@
 
     each(band_blocks, clear)
 
-    for c in range(panels):
-
-        def forward(i, c=c):
-            copy = across(i + 1, c)
-            copy.wait_recv()
-            copy.start()
-
-        each(onward, forward)
+    def pass_on(t):
+        for c in range(panels):
+
+            @pl.when(spot > t)
+            def _(c=c):
+                across(spot - 1 - t, c).wait_recv()
+                pl.when(above)(lambda: up(t + 1, c).start())
+                across(spot - 1 - t, c).start()
+
+            @pl.when(spot + t < half - 1)
+            def _(c=c):
+                across(spot + 1 + t, c).wait_recv()
+                pl.when(below)(lambda: down(t + 1, c).start())
+                across(spot + 1 + t, c).start()
+
+    each(half - 1, pass_on)
 
     fetch_right.wait()
     each(bands - 1, lambda s: send_right(s, other(s)).wait_recv())
@@ -227,9 +238,14 @@
     for p in range(panels):
         each(bands - 1, lambda s, p=p: send_out(s, other(s), p).wait_recv())
         keep_own(p).wait()
-    for c in range(panels):
-        each(onward, lambda i, c=c: along(i, c).wait_send())
-        each(onward + 1, lambda i, c=c: across(i, c).wait_send())
+
+    def settle(t):
+        for c in range(panels):
+            across(t, c).wait_send()
+            pl.when(above & (t <= spot))(lambda c=c: up(t, c).wait_send())
+            pl.when(below & (t < half - spot))(lambda c=c: down(t, c).wait_send())
+
+    each(half, settle)
     each(bands - 1, lambda s: send_right(s, layer).wait_send())
     each(bands - 1, lambda s: send_total(s, layer).wait_send())
     for p in range(panels):
@@ -263,6 +279,7 @@
                 dma((5,)),
                 dma((cycle // 2, panels)),
                 dma((cycle // 2, panels)),
+                dma((cycle // 2, panels)),
                 dma((bands,)),
                 dma((cycle, panels)),
                 dma((bands,)),

time: 26 us -> 27.6 us (1.062)
  Pallas kernels: 24.1 us -> 25.8 us
    pallas_call x1, Pallas kernels: 24.1 us -> 25.8 us  [per_device(): pl.pallas_call(functools.partial(kernel, cycle, bands, panels, per_band),...]
where the time goes in v5:
time: 27.6 us; the launch traced here: 27.4 us
  Pallas kernels  25.8 us (93%)
  local copies, waits for them, and re-layouts  1.67 us (6%)
    pallas_call x1, Pallas kernels, per_device(): pl.pallas_call(functools.partial(kernel, cycle, bands, panels, per_band),...  25.8 us
    unnamed x1, local copies, waits for them, and re-layouts  1.67 us

profile of v5, /device:TPU:0, one launch (start us, length us, event | category | flops | bytes accessed | tf_op | source)
XLA Modules:
  0.0 27.4 jit_solution(17116180338230038035)
XLA Ops:
  0.0 25.8 %shard_map.46 = bf16[2,4,1,128,128]{4,3,2,1,0:T(8,128)(2,1)} custom-call(bf16[256,128]{1,0:T(8,128)(2,1)} %bitcast.2, s32[1,1,2]{2,1,0:T(1,128)} %bitcast.3, s32[2,1,4]{2,1,0:T(1,128)} %kept_hbm.1, s32[2,4,128]{2,1,0:T(4,128)} %mask_hbm.1), custom_call_target="tpu_custom_call" | custom-call | tf_op jit(solution)/shard_map/pallas_call | solution.py:265
  25.8 1.7 %copy.6 = bf16[2,4,1,128,128]{4,3,2,1,0:T(8,128)(2,1)} copy(bf16[2,4,1,128,128]{4,3,2,1,0:T(8,128)(2,1)} %shard_map.46) | data formatting | bytes 524288

commit v6 on v4

--- a/solution.py
+++ b/solution.py
@@ -26,7 +26,7 @@
 def kernel(
     cycle, bands, panels, per_band, tiles_hbm, rows_hbm, kept_hbm, mask_hbm, out_ref,
     left, right, expanded, totals, stage, rows_ref, kept_ref, mask_ref,
-    local, line_send, pair_send, layer_send, left_recv, right_recv,
+    local, left_send, layer_send, left_recv, right_recv,
     total_send, total_recv, out_send, out_recv, keep_sem,
 ):
     tile = tiles_hbm.shape[1]
@@ -34,23 +34,14 @@
     body = panels * per_band * tile
     band_blocks = panels * cycle // bands
     owners = band_blocks // panels
-    lanes = owners // 2
-    onward = cycle // 2 - 1
     me, layer = lax.axis_index("blk"), lax.axis_index("layer")
-    side = lax.rem(me, 2)
-    pair = me + 1 - 2 * side
-    own_band, own_lane = me // owners, lax.rem(me // 2, lanes)
+    own_band = me // owners
 
     def other(s):
         return lax.rem(layer + 1 + s, bands)
 
-    def owner_at(i, which):
-        band = xor(own_band, i // lanes, bands)
-        return 2 * (band * lanes + lax.rem(own_lane + lax.rem(i, lanes), lanes)) + which
-
-    def target_at(i):
-        band = xor(own_band, i // lanes, bands)
-        return 2 * (band * lanes + lax.rem(own_lane + lanes - lax.rem(i, lanes), lanes)) + side
+    def target_at(s):
+        return lax.rem(me + 1 + s, cycle)
 
     fetch_rows = pltpu.make_async_copy(rows_hbm, rows_ref, local.at[0])
     fetch_tiles = pltpu.make_async_copy(tiles_hbm, left.at[me, pl.ds(NOTE, body)], local.at[1])
@@ -63,8 +54,7 @@
     def greet(peer):
         pl.semaphore_signal(barrier, inc=1, device_id=peer, device_id_type=MESH)
 
-    greet({"blk": pair})
-    each(onward, lambda i: greet({"blk": target_at(i + 1)}))
+    each(cycle - 1, lambda s: greet({"blk": target_at(s)}))
     each(bands - 1, lambda s: greet({"layer": other(s)}))
     for fetch in (fetch_rows, fetch_tiles, fetch_right, fetch_kept, fetch_mask):
         fetch.start()
@@ -79,16 +69,12 @@
     left[me, 0:NOTE, :] = note
     right[layer, 0:NOTE, :] = note
     fetch_tiles.wait()
-    pl.semaphore_wait(barrier, onward + bands)
-
-    part = per_band * tile
-    chunks = [(NOTE + c * part if c else 0, part if c else NOTE + part) for c in range(panels)]
-
-    def send_left(slot, target, send_sem, c):
-        rows = pl.ds(*chunks[c])
-        return pltpu.make_async_remote_copy(
-            src_ref=left.at[slot, rows], dst_ref=left.at[slot, rows], send_sem=send_sem,
-            recv_sem=left_recv.at[slot, c], device_id={"blk": target}, device_id_type=MESH,
+    pl.semaphore_wait(barrier, cycle + bands - 2)
+
+    def send_left(s, slot):
+        return pltpu.make_async_remote_copy(
+            src_ref=left.at[slot], dst_ref=left.at[slot], send_sem=left_send.at[s],
+            recv_sem=left_recv.at[slot], device_id={"blk": target_at(s)}, device_id_type=MESH,
         )
 
     def send_right(s, band):
@@ -97,15 +83,7 @@
             recv_sem=right_recv.at[band], device_id={"layer": other(s)}, device_id_type=MESH,
         )
 
-    def along(i, c):
-        return send_left(me, target_at(i + 1), line_send.at[i, c], c)
-
-    def across(i, c):
-        return send_left(owner_at(i, side), pair, pair_send.at[i, c], c)
-
-    for c in range(panels):
-        across(0, c).start()
-        each(onward, lambda i, c=c: along(i, c).start())
+    each(cycle - 1, lambda s: send_left(s, me).start())
     each(bands - 1, lambda s: send_right(s, layer).start())
 
     def clear(i):
@@ -114,25 +92,18 @@
 
     each(band_blocks, clear)
 
-    for c in range(panels):
-
-        def forward(i, c=c):
-            copy = across(i + 1, c)
-            copy.wait_recv()
-            copy.start()
-
-        each(onward, forward)
-
     fetch_right.wait()
     each(bands - 1, lambda s: send_right(s, other(s)).wait_recv())
 
     def product(d):
-        def arrive(h):
-            for c in range(panels):
-                send_left(owner_at(d * lanes + h, 1 - side), pair, pair_send.at[0, c], c).wait_recv()
-
-        each(lanes, arrive)
         q = xor(own_band, d, bands)
+
+        def arrive(o):
+            @pl.when(q * owners + o != me)
+            def _():
+                send_left(0, q * owners + o).wait_recv()
+
+        each(owners, arrive)
         wanted = right[q, 0:NOTE, :].astype(jnp.float32)
         for p in range(panels):
             for k in range(per_band):
@@ -227,9 +198,7 @@
     for p in range(panels):
         each(bands - 1, lambda s, p=p: send_out(s, other(s), p).wait_recv())
         keep_own(p).wait()
-    for c in range(panels):
-        each(onward, lambda i, c=c: along(i, c).wait_send())
-        each(onward + 1, lambda i, c=c: across(i, c).wait_send())
+    each(cycle - 1, lambda s: send_left(s, me).wait_send())
     each(bands - 1, lambda s: send_right(s, layer).wait_send())
     each(bands - 1, lambda s: send_total(s, layer).wait_send())
     for p in range(panels):
@@ -261,10 +230,9 @@
                 pltpu.SMEM(kept_rows.shape, jnp.int32),
                 pltpu.VMEM(prune_mask.shape, jnp.int32),
                 dma((5,)),
-                dma((cycle // 2, panels)),
-                dma((cycle // 2, panels)),
-                dma((bands,)),
-                dma((cycle, panels)),
+                dma((cycle,)),
+                dma((bands,)),
+                dma((cycle,)),
                 dma((bands,)),
                 dma((bands,)),
                 dma((bands,)),

time: 26 us -> 26.7 us (1.027)
  the two profiles are of different devices: /device:TPU:0 before, /device:TPU:11 now
where the time goes in v6:
time: 26.7 us; the launch traced here: 26.5 us
  Pallas kernels  24.8 us (93%)
  local copies, waits for them, and re-layouts  1.67 us (6%)
    pallas_call x1, Pallas kernels, per_device(): pl.pallas_call(functools.partial(kernel, cycle, bands, panels, per_band),...  24.8 us
    unnamed x1, local copies, waits for them, and re-layouts  1.67 us

profile of v6, /device:TPU:11, one launch (start us, length us, event | category | flops | bytes accessed | tf_op | source)
XLA Modules:
  0.0 26.5 jit_solution(17626971174590174107)
XLA Ops:
  0.0 24.8 %shard_map.46 = bf16[2,4,1,128,128]{4,3,2,1,0:T(8,128)(2,1)} custom-call(bf16[256,128]{1,0:T(8,128)(2,1)} %bitcast.2, s32[1,1,2]{2,1,0:T(1,128)} %bitcast.3, s32[2,1,4]{2,1,0:T(1,128)} %kept_hbm.1, s32[2,4,128]{2,1,0:T(4,128)} %mask_hbm.1), custom_call_target="tpu_custom_call" | custom-call | tf_op jit(solution)/shard_map/pallas_call | solution.py:218
  24.8 1.7 %copy.6 = bf16[2,4,1,128,128]{4,3,2,1,0:T(8,128)(2,1)} copy(bf16[2,4,1,128,128]{4,3,2,1,0:T(8,128)(2,1)} %shard_map.46) | data formatting | bytes 524288

commit v7 on v4

--- a/solution.py
+++ b/solution.py
@@ -44,12 +44,15 @@
     def other(s):
         return lax.rem(layer + 1 + s, bands)
 
+    def band_at(i):
+        return xor(own_band, lax.rem(bands - i, bands), bands)
+
     def owner_at(i, which):
-        band = xor(own_band, i // lanes, bands)
+        band = band_at(i // lanes)
         return 2 * (band * lanes + lax.rem(own_lane + lax.rem(i, lanes), lanes)) + which
 
     def target_at(i):
-        band = xor(own_band, i // lanes, bands)
+        band = band_at(i // lanes)
         return 2 * (band * lanes + lax.rem(own_lane + lanes - lax.rem(i, lanes), lanes)) + side
 
     fetch_rows = pltpu.make_async_copy(rows_hbm, rows_ref, local.at[0])
@@ -132,7 +135,7 @@
                 send_left(owner_at(d * lanes + h, 1 - side), pair, pair_send.at[0, c], c).wait_recv()
 
         each(lanes, arrive)
-        q = xor(own_band, d, bands)
+        q = band_at(d)
         wanted = right[q, 0:NOTE, :].astype(jnp.float32)
         for p in range(panels):
             for k in range(per_band):

time: 26 us -> 26.8 us (1.031)
  Pallas kernels: 24.1 us -> 24.9 us
    pallas_call x1, Pallas kernels: 24.1 us -> 24.9 us  [per_device(): pl.pallas_call(functools.partial(kernel, cycle, bands, panels, per_band),...]
where the time goes in v7:
time: 26.8 us; the launch traced here: 26.6 us
  Pallas kernels  24.9 us (93%)
  local copies, waits for them, and re-layouts  1.67 us (6%)
    pallas_call x1, Pallas kernels, per_device(): pl.pallas_call(functools.partial(kernel, cycle, bands, panels, per_band),...  24.9 us
    unnamed x1, local copies, waits for them, and re-layouts  1.67 us

profile of v7, /device:TPU:0, one launch (start us, length us, event | category | flops | bytes accessed | tf_op | source)
XLA Modules:
  0.0 26.6 jit_solution(13969073965669129991)
XLA Ops:
  0.0 24.9 %shard_map.46 = bf16[2,4,1,128,128]{4,3,2,1,0:T(8,128)(2,1)} custom-call(bf16[256,128]{1,0:T(8,128)(2,1)} %bitcast.2, s32[1,1,2]{2,1,0:T(1,128)} %bitcast.3, s32[2,1,4]{2,1,0:T(1,128)} %kept_hbm.1, s32[2,4,128]{2,1,0:T(4,128)} %mask_hbm.1), custom_call_target="tpu_custom_call" | custom-call | tf_op jit(solution)/shard_map/pallas_call | solution.py:252
  24.9 1.7 %copy.6 = bf16[2,4,1,128,128]{4,3,2,1,0:T(8,128)(2,1)} copy(bf16[2,4,1,128,128]{4,3,2,1,0:T(8,128)(2,1)} %shard_map.46) | data formatting | bytes 524288

commit v8 on v4

--- a/solution.py
+++ b/solution.py
@@ -26,7 +26,7 @@
 def kernel(
     cycle, bands, panels, per_band, tiles_hbm, rows_hbm, kept_hbm, mask_hbm, out_ref,
     left, right, expanded, totals, stage, rows_ref, kept_ref, mask_ref,
-    local, line_send, pair_send, layer_send, left_recv, right_recv,
+    local, line_send, direct_send, pair_send, layer_send, left_recv, right_recv,
     total_send, total_recv, out_send, out_recv, keep_sem,
 ):
     tile = tiles_hbm.shape[1]
@@ -65,6 +65,7 @@
 
     greet({"blk": pair})
     each(onward, lambda i: greet({"blk": target_at(i + 1)}))
+    each(onward, lambda i: greet({"blk": target_at(i + 1) + pair - me}))
     each(bands - 1, lambda s: greet({"layer": other(s)}))
     for fetch in (fetch_rows, fetch_tiles, fetch_right, fetch_kept, fetch_mask):
         fetch.start()
@@ -79,7 +80,7 @@
     left[me, 0:NOTE, :] = note
     right[layer, 0:NOTE, :] = note
     fetch_tiles.wait()
-    pl.semaphore_wait(barrier, onward + bands)
+    pl.semaphore_wait(barrier, 2 * onward + bands)
 
     part = per_band * tile
     chunks = [(NOTE + c * part if c else 0, part if c else NOTE + part) for c in range(panels)]
@@ -100,12 +101,17 @@
     def along(i, c):
         return send_left(me, target_at(i + 1), line_send.at[i, c], c)
 
+    def direct(i, c):
+        return send_left(me, target_at(i + 1) + pair - me, direct_send.at[i, c], c)
+
     def across(i, c):
         return send_left(owner_at(i, side), pair, pair_send.at[i, c], c)
 
     for c in range(panels):
         across(0, c).start()
         each(onward, lambda i, c=c: along(i, c).start())
+        if c:
+            each(onward, lambda i, c=c: direct(i, c).start())
     each(bands - 1, lambda s: send_right(s, layer).start())
 
     def clear(i):
@@ -114,14 +120,12 @@
 
     each(band_blocks, clear)
 
-    for c in range(panels):
-
-        def forward(i, c=c):
-            copy = across(i + 1, c)
-            copy.wait_recv()
-            copy.start()
-
-        each(onward, forward)
+    def forward(i):
+        copy = across(i + 1, 0)
+        copy.wait_recv()
+        copy.start()
+
+    each(onward, forward)
 
     fetch_right.wait()
     each(bands - 1, lambda s: send_right(s, other(s)).wait_recv())
@@ -130,6 +134,12 @@
         def arrive(h):
             for c in range(panels):
                 send_left(owner_at(d * lanes + h, 1 - side), pair, pair_send.at[0, c], c).wait_recv()
+            for c in range(1, panels):
+                source = owner_at(d * lanes + h, side)
+
+                @pl.when(source != me)
+                def _(c=c, source=source):
+                    send_left(source, pair, pair_send.at[0, c], c).wait_recv()
 
         each(lanes, arrive)
         q = xor(own_band, d, bands)
@@ -229,7 +239,9 @@
         keep_own(p).wait()
     for c in range(panels):
         each(onward, lambda i, c=c: along(i, c).wait_send())
-        each(onward + 1, lambda i, c=c: across(i, c).wait_send())
+        each(1 if c else onward + 1, lambda i, c=c: across(i, c).wait_send())
+        if c:
+            each(onward, lambda i, c=c: direct(i, c).wait_send())
     each(bands - 1, lambda s: send_right(s, layer).wait_send())
     each(bands - 1, lambda s: send_total(s, layer).wait_send())
     for p in range(panels):
@@ -263,6 +275,7 @@
                 dma((5,)),
                 dma((cycle // 2, panels)),
                 dma((cycle // 2, panels)),
+                dma((cycle // 2, panels)),
                 dma((bands,)),
                 dma((cycle, panels)),
                 dma((bands,)),

time: 26 us -> 26.3 us (1.012)
  Pallas kernels: 24.1 us -> 24.4 us
    pallas_call x1, Pallas kernels: 24.1 us -> 24.4 us  [per_device(): pl.pallas_call(functools.partial(kernel, cycle, bands, panels, per_band),...]
where the time goes in v8:
time: 26.3 us; the launch traced here: 26.1 us
  Pallas kernels  24.4 us (93%)
  local copies, waits for them, and re-layouts  1.67 us (6%)
    pallas_call x1, Pallas kernels, per_device(): pl.pallas_call(functools.partial(kernel, cycle, bands, panels, per_band),...  24.4 us
    unnamed x1, local copies, waits for them, and re-layouts  1.67 us

profile of v8, /device:TPU:0, one launch (start us, length us, event | category | flops | bytes accessed | tf_op | source)
XLA Modules:
  0.0 26.1 jit_solution(5260157104866428978)
XLA Ops:
  0.0 24.4 %shard_map.46 = bf16[2,4,1,128,128]{4,3,2,1,0:T(8,128)(2,1)} custom-call(bf16[256,128]{1,0:T(8,128)(2,1)} %bitcast.2, s32[1,1,2]{2,1,0:T(1,128)} %bitcast.3, s32[2,1,4]{2,1,0:T(1,128)} %kept_hbm.1, s32[2,4,128]{2,1,0:T(4,128)} %mask_hbm.1), custom_call_target="tpu_custom_call" | custom-call | tf_op jit(solution)/shard_map/pallas_call | solution.py:261
  24.4 1.7 %copy.6 = bf16[2,4,1,128,128]{4,3,2,1,0:T(8,128)(2,1)} copy(bf16[2,4,1,128,128]{4,3,2,1,0:T(8,128)(2,1)} %shard_map.46) | data formatting | bytes 524288

commit v9 on v4

--- a/solution.py
+++ b/solution.py
@@ -250,7 +250,7 @@
             functools.partial(kernel, cycle, bands, panels, per_band),
             out_shape=jax.ShapeDtypeStruct((panels, bands, per_layer, tile, tile), jnp.bfloat16),
             in_specs=[hbm] * 4,
-            out_specs=hbm,
+            out_specs=pl.BlockSpec(memory_space=pltpu.VMEM),
             scratch_shapes=[
                 pltpu.VMEM((cycle, message, tile), jnp.bfloat16),
                 pltpu.VMEM((bands, message, tile), jnp.bfloat16),
@@ -273,7 +273,7 @@
                 dma((panels,)),
             ],
             compiler_params=pltpu.CompilerParams(
-                collective_id=0, has_side_effects=True, vmem_limit_bytes=63 * 1024 * 1024
+                collective_id=0, has_side_effects=True, vmem_limit_bytes=32 * 1024 * 1024
             ),
         )(
             tile_values.reshape(panels * per_band * tile, tile),

time: 26 us -> 27.2 us (1.046)
  local copies, waits for them, and re-layouts: 1.67 us -> 2.91 us
    unnamed x1 -> x9, local copies, waits for them, and re-layouts: 1.67 us -> 2.91 us
where the time goes in v9:
time: 27.2 us; the launch traced here: 27 us
  Pallas kernels  24 us (88%)
  local copies, waits for them, and re-layouts  2.91 us (11%)
    pallas_call x1, Pallas kernels, per_device(): pl.pallas_call(functools.partial(kernel, cycle, bands, panels, per_band),...  24 us
    unnamed x9, local copies, waits for them, and re-layouts  2.91 us

profile of v9, /device:TPU:0, one launch (start us, length us, event | category | flops | bytes accessed | tf_op | source)
XLA Modules:
  0.0 27.0 jit_solution(8269767371574054518)
XLA Ops:
  0.0 0.0 copy-start.2
  0.0 0.0 copy-start.3
  0.0 0.7 %copy-done.2 = s32[2,1,4]{2,1,0:T(1,128)S(1)} copy-done((s32[2,1,4]{2,1,0:T(1,128)S(1)}, s32[2,1,4]{2,1,0:T(1,128)}, u32[]{:S(2)}) %copy-start.2) | copy-done | bytes 56
  0.7 0.0 copy-done.3
  0.7 0.0 copy-start
  0.7 0.8 %copy-done = bf16[2,1,1,128,128]{4,3,2,1,0:T(8,128)(2,1)S(1)} copy-done((bf16[2,1,1,128,128]{4,3,2,1,0:T(8,128)(2,1)S(1)}, bf16[2,1,1,128,128]{4,3,2,1,0:T(8,128)(2,1)}, u32[]{:S(2)}) %copy-start) | copy-done | bytes 65560
  1.5 0.0 copy-start.1
  1.5 0.7 %copy-done.1 = s32[2,4,128]{2,1,0:T(4,128)S(1)} copy-done((s32[2,4,128]{2,1,0:T(4,128)S(1)}, s32[2,4,128]{2,1,0:T(4,128)}, u32[]{:S(2)}) %copy-start.1) | copy-done | bytes 4120
  2.2 24.0 %shard_map.46 = bf16[2,4,1,128,128]{4,3,2,1,0:T(8,128)(2,1)S(1)} custom-call(bf16[256,128]{1,0:T(8,128)(2,1)S(1)} %bitcast.2, s32[1,1,2]{2,1,0:T(1,128)S(1)} %bitcast.3, s32[2,1,4]{2,1,0:T(1,128)S(1)} %copy-done.2, s32[2,4,128]{2,1,0:T(4,128)S(1)} %copy-done.1), custom_call_target="tpu_custom_call" | custom-call | tf_op jit(solution)/shard_map/pallas_call | solution.py:249
  26.3 0.7 %copy.6 = bf16[2,4,1,128,128]{4,3,2,1,0:T(8,128)(2,1)} copy(bf16[2,4,1,128,128]{4,3,2,1,0:T(8,128)(2,1)S(1)} %shard_map.46) | data formatting | bytes 524288
Async XLA Ops:
  0.0 0.7 %copy-start.2 = (s32[2,1,4]{2,1,0:T(1,128)S(1)}, s32[2,1,4]{2,1,0:T(1,128)}, u32[]{:S(2)}) copy-start(s32[2,1,4]{2,1,0:T(1,128)} %kept_hbm.1) | copy-start | bytes 100
  0.0 0.7 %copy-start.3 = (s32[2,1,1]{0,2,1:T(1,128)S(1)}, s32[2,1,1]{0,2,1:T(1,128)}, u32[]{:S(2)}) copy-start(s32[2,1,1]{0,2,1:T(1,128)} %param.5) | copy-start | bytes 28
  0.7 0.8 %copy-start = (bf16[2,1,1,128,128]{4,3,2,1,0:T(8,128)(2,1)S(1)}, bf16[2,1,1,128,128]{4,3,2,1,0:T(8,128)(2,1)}, u32[]{:S(2)}) copy-start(bf16[2,1,1,128,128]{4,3,2,1,0:T(8,128)(2,1)} %param.4) | copy-start | bytes 196612
  1.5 0.7 %copy-start.1 = (s32[2,4,128]{2,1,0:T(4,128)S(1)}, s32[2,4,128]{2,1,0:T(4,128)}, u32[]{:S(2)}) copy-start(s32[2,4,128]{2,1,0:T(4,128)} %mask_hbm.1) | copy-start | bytes 12292

commit v10 on v4

--- a/solution.py
+++ b/solution.py
@@ -81,8 +81,7 @@
     fetch_tiles.wait()
     pl.semaphore_wait(barrier, onward + bands)
 
-    part = per_band * tile
-    chunks = [(NOTE + c * part if c else 0, part if c else NOTE + part) for c in range(panels)]
+    chunks = [(0, NOTE + body)]
 
     def send_left(slot, target, send_sem, c):
         rows = pl.ds(*chunks[c])
@@ -103,7 +102,7 @@
     def across(i, c):
         return send_left(owner_at(i, side), pair, pair_send.at[i, c], c)
 
-    for c in range(panels):
+    for c in range(len(chunks)):
         across(0, c).start()
         each(onward, lambda i, c=c: along(i, c).start())
     each(bands - 1, lambda s: send_right(s, layer).start())
@@ -114,7 +113,7 @@
 
     each(band_blocks, clear)
 
-    for c in range(panels):
+    for c in range(len(chunks)):
 
         def forward(i, c=c):
             copy = across(i + 1, c)
@@ -128,7 +127,7 @@
 
     def product(d):
         def arrive(h):
-            for c in range(panels):
+            for c in range(len(chunks)):
                 send_left(owner_at(d * lanes + h, 1 - side), pair, pair_send.at[0, c], c).wait_recv()
 
         each(lanes, arrive)
@@ -227,7 +226,7 @@
     for p in range(panels):
         each(bands - 1, lambda s, p=p: send_out(s, other(s), p).wait_recv())
         keep_own(p).wait()
-    for c in range(panels):
+    for c in range(len(chunks)):
         each(onward, lambda i, c=c: along(i, c).wait_send())
         each(onward + 1, lambda i, c=c: across(i, c).wait_send())
     each(bands - 1, lambda s: send_right(s, layer).wait_send())

time: 26 us -> 26 us (level)
  no operation moved by 1% of the time
where the time goes in v10:
time: 26 us; the launch traced here: 25.8 us
  Pallas kernels  24.1 us (93%)
  local copies, waits for them, and re-layouts  1.67 us (6%)
    pallas_call x1, Pallas kernels, per_device(): pl.pallas_call(functools.partial(kernel, cycle, bands, panels, per_band),...  24.1 us
    unnamed x1, local copies, waits for them, and re-layouts  1.67 us

profile of v10, /device:TPU:0, one launch (start us, length us, event | category | flops | bytes accessed | tf_op | source)
XLA Modules:
  0.0 25.8 jit_solution(17713048599843363473)
XLA Ops:
  0.0 24.1 %shard_map.46 = bf16[2,4,1,128,128]{4,3,2,1,0:T(8,128)(2,1)} custom-call(bf16[256,128]{1,0:T(8,128)(2,1)} %bitcast.2, s32[1,1,2]{2,1,0:T(1,128)} %bitcast.3, s32[2,1,4]{2,1,0:T(1,128)} %kept_hbm.1, s32[2,4,128]{2,1,0:T(4,128)} %mask_hbm.1), custom_call_target="tpu_custom_call" | custom-call | tf_op jit(solution)/shard_map/pallas_call | solution.py:248
  24.1 1.7 %copy.6 = bf16[2,4,1,128,128]{4,3,2,1,0:T(8,128)(2,1)} copy(bf16[2,4,1,128,128]{4,3,2,1,0:T(8,128)(2,1)} %shard_map.46) | data formatting | bytes 524288
